TPU v7x, 256 devices: a whole 4x4x8 slice. The times are simulated.
256 devices in a mesh: space: 16 (over z_hi, x), chan: 16 (over y, z_lo, core).
Axes of the slice: x: 4, y: 4, z: 8 (z_hi: 4, z_lo: 2; z = z_hi * 2 + z_lo), core: 2. Of those that a mesh axis runs over, the one named last changes fastest.
Arguments:
- features: bfloat16 [49, 128, 2048], P(None, 'chan', 'space'), may hold values from -6 to 6
- ghost_index: int32 [2, 1024], P(None, 'space'), may hold values from 0 to 127
- edge_src: int32 [4096], P('space'), may hold values from 0 to 255
- edge_dst: int32 [4096], P('space'), may hold values from 0 to 127
- edge_count: int32 [16], P('space'), may hold values from 64 to 256, as said below
- rotation: bfloat16 [235, 4096], P(None, 'space'), may hold values from -3 to 3
- distance: float32 [4096], P('space'), may hold values from 1 to 11
- edge_angle: float32 [2, 4096], P(None, 'space'), may hold values from -3.140625 to 3.140625
- radial_weight: bfloat16 [512, 128], replicated, may hold values from -1 to 1
- conv_zero: bfloat16 [7, 128, 896], P(None, 'chan'), may hold values from -0.1875 to 0.1875
- conv_one: bfloat16 [2, 6, 128, 768], P(None, None, 'chan'), may hold values from -0.15625 to 0.15625
- conv_two: bfloat16 [2, 5, 128, 640], P(None, None, 'chan'), may hold values from -0.15625 to 0.15625
- energy_weight: float32 [7, 128], P(None, 'chan'), may hold values from -0.1875 to 0.1875
Outputs:
- atom_energy: float32 [2048], P('space')
- forces: float32 [3, 2048], P(None, 'space')
Inputs may be any that keep to these rules, and one draw needn't show every extreme that they name: `edge_count`: at least one slab has all 256 slots live.
All inputs are finite; a program needn't handle non-finite values.
Results may differ from a plain program's by a relative error of at most 0.014.
Values may be sent and summed in bfloat16 or wider, within the bound.
A program may use at most 64 MiB of HBM per device.

v0:
```python
import jax
import jax.numpy as jnp
from jax import lax
from jax.experimental import pallas as pl
from jax.experimental.pallas import tpu as pltpu
from jax.sharding import PartitionSpec as P

MESH = pl.DeviceIdType.MESH
F32 = jnp.float32
BF16 = jnp.bfloat16
NC = 16
CHUNKS = ((0, 64), (64, 96), (160, 80))
HEIGHT = [min(2 * l + 1, 5) for l in range(7)]
OFFSET = [sum(HEIGHT[m] * (2 * m + 1) for m in range(l)) for l in range(7)]
FIRST = (0, 7, 13, 19, 24)
LEAST = (0, 1, 1, 2, 2)


def row_of(degree, order):
    return FIRST[order] + degree - LEAST[order]


def padded_row(row):
    return row if row < 7 else row + 1


def dot(a, b):
    return jnp.dot(a, b, preferred_element_type=F32)


def dot_nt(a, b):
    return lax.dot_general(a, b, (((1,), (1,)), ((), ())), preferred_element_type=F32)


def split(x):
    hi = x.astype(BF16)
    return hi, (x - hi.astype(F32)).astype(BF16)


def kernel(
    feat, gidx, esrc, edst, count, rot, dist, ang, radial, wzero, wone, wtwo, eweight,
    energy_out, force_out,
    mine, mine_g, ghost, ghost_g, wz, w1, w2, rf, r3, s3, t3, snd, every, gate, x, ob, orecv,
    pf, pt, fcoef, nconst, ewcol, red, fsend, frecv,
    g_send, g_recv, w_send, w_recv, a_send, a_recv, o_send, o_recv, r_send, r_recv, f_send, f_recv,
):
    space = lax.axis_index("space")
    chan = lax.axis_index("chan")
    n_space = lax.axis_size("space")
    after = lax.rem(space + 1, n_space)
    before = lax.rem(space + n_space - 1, n_space)
    core = lax.rem(chan, 2)
    other = 1 - core
    sibling = chan + 1 - 2 * core

    def remote(src, dst, send, recv, where):
        return pltpu.make_async_remote_copy(
            src_ref=src, dst_ref=dst, send_sem=send, recv_sem=recv, device_id=where, device_id_type=MESH
        )

    barrier = pltpu.get_barrier_semaphore()

    def greet(d, carry):
        pl.semaphore_signal(barrier, inc=1, device_id=(space, lax.rem(chan + d, NC)), device_id_type=MESH)
        return carry

    lax.fori_loop(1, NC, greet, 0)
    pl.semaphore_signal(barrier, inc=1, device_id=(after, chan), device_id_type=MESH)
    pl.semaphore_signal(barrier, inc=1, device_id=(before, chan), device_id_type=MESH)

    own = feat[...].astype(F32).reshape(392, 128)
    fcoef[...] = own
    mine[0:392, :] = own.astype(BF16)
    mine[384:400, :] = jnp.concatenate([own[384:392], jnp.zeros((8, 128), F32)], axis=0).astype(BF16)
    mine_g[...] = jnp.zeros((8, 128), jnp.int32)
    mine_g[0:2, 0:64] = gidx[...]
    pl.semaphore_wait(barrier, NC + 1)

    exchange = [
        remote(mine, ghost.at[0], g_send.at[0], g_recv.at[0], (after, chan)),
        remote(mine, ghost.at[1], g_send.at[1], g_recv.at[1], (before, chan)),
        remote(mine_g, ghost_g.at[0], g_send.at[2], g_recv.at[2], (after, chan)),
        remote(mine_g, ghost_g.at[1], g_send.at[3], g_recv.at[3], (before, chan)),
    ]
    for copy in exchange:
        copy.start()

    wz[core] = jnp.concatenate(
        [wzero[...].astype(F32).reshape(56, 896), jnp.zeros((8, 896), F32)], axis=0
    ).astype(BF16)
    w1[core] = wone[...].astype(F32).reshape(96, 768).astype(BF16)
    w2[core] = wtwo[...].astype(F32).reshape(80, 640).astype(BF16)
    weights = [
        remote(w.at[core], w.at[core], w_send.at[i], w_recv.at[i], (space, sibling))
        for i, w in enumerate((wz, w1, w2))
    ]
    for copy in weights:
        copy.start()

    rf[0:235, :] = rot[...].astype(F32)

    def spread(i, carry):
        for j in range(5):
            row = i * 5 + j
            line = rf[pl.ds(row, 1), :]
            r3[0, row] = jnp.broadcast_to(line[:, :128], (8, 128))
            r3[1, row] = jnp.broadcast_to(line[:, 128:], (8, 128))
        return carry

    lax.fori_loop(0, 47, spread, 0)

    atom_row = lax.broadcasted_iota(jnp.int32, (128, 256), 0)
    source = esrc[...]
    target_hot = (edst[...] == atom_row).astype(F32)
    source_hot = (source == atom_row).astype(F32)
    nconst[0] = source_hot.astype(BF16)
    nconst[3] = target_hot.astype(BF16)
    base_coeffs = dot(mine[...], nconst[0])

    live = (lax.broadcasted_iota(jnp.int32, (1, 128), 1) + core * 128 < count[...]).astype(F32)
    center = 12.0 * lax.broadcasted_iota(jnp.int32, (512, 128), 0).astype(F32) / 511.0
    grid = dist[pl.ds(core, 1), :] - center
    basis = jnp.exp(-2.0 * grid * grid)
    slope = -4.0 * grid * basis
    both = jnp.concatenate([basis.astype(BF16), slope.astype(BF16)], axis=1)
    radial_out = lax.dot_general(
        radial[...], both, (((0,), (0,)), ((), ())), preferred_element_type=F32
    )
    preact = radial_out[:, :128]
    sigma = jax.nn.sigmoid(preact)
    gate[0] = preact * sigma * live
    gate[1] = sigma * (1.0 + preact * (1.0 - sigma)) * live * radial_out[:, 128:]

    eye = (
        lax.broadcasted_iota(jnp.int32, (8, 8), 0) == lax.broadcasted_iota(jnp.int32, (8, 8), 1)
    ).astype(F32)
    for degree in range(7):
        column = jnp.sum(eweight[degree : degree + 1, :] * eye, axis=1, keepdims=True)
        ewcol[degree] = jnp.broadcast_to(column, (8, 128))

    polar, azimuth = ang[0:1, :], ang[1:2, :]
    unit = [jnp.sin(polar) * jnp.cos(azimuth), jnp.sin(polar) * jnp.sin(azimuth), jnp.cos(polar)]

    slot_row = lax.broadcasted_iota(jnp.int32, (64, 256), 0)
    atom_lane = lax.broadcasted_iota(jnp.int32, (128, 64), 0)
    for copy in exchange:
        copy.wait_recv()
    coeffs = base_coeffs
    for side in range(2):
        slot_hot = (source - (128 + 64 * side) == slot_row).astype(F32).astype(BF16)
        lent_hot = (ghost_g[side, side : side + 1, 0:64] == atom_lane).astype(F32).astype(BF16)
        nconst[1 + side] = dot(lent_hot, slot_hot).astype(BF16)
        coeffs = coeffs + dot(ghost[side], nconst[1 + side])
    s3[0] = coeffs[0:392, :128].reshape(49, 8, 128)
    s3[1] = coeffs[0:392, 128:].reshape(49, 8, 128)

    def transfers(d, g):
        first, rows = CHUNKS[g]
        to = lax.rem(chan + d, NC)
        return remote(
            snd.at[lax.rem(to, 2), pl.ds(first, rows)],
            every.at[chan, pl.ds(first, rows)],
            a_send.at[d - 1, g],
            a_recv.at[d - 1, g],
            (space, to),
        )

    t3[:, 7] = jnp.zeros((2, 8, 128), F32)
    for g in range(3):
        for order in ((0,), (1, 2), (3, 4))[g]:
            for degree in range(LEAST[order], 7):
                width = 2 * degree + 1
                at = OFFSET[degree] + order * width
                row = padded_row(row_of(degree, order))
                for half in range(2):
                    t3[half, row] = jnp.sum(
                        r3[half, at : at + width] * s3[half, degree * degree : (degree + 1) ** 2], axis=0
                    )
        first, rows = CHUNKS[g]
        for half in range(2):
            snd[half, first : first + rows] = (
                t3[half, first // 8 : (first + rows) // 8].reshape(rows, 128).astype(BF16)
            )
        every[chan, first : first + rows] = snd[core, first : first + rows]

        def launch(d, carry):
            transfers(d, g).start()
            return carry

        lax.fori_loop(1, NC, launch, 0)

    for copy in weights:
        copy.wait_recv()
    for g in range(3):

        def arrive(d, carry):
            transfers(d, g).wait_recv()
            return carry

        lax.fori_loop(1, NC, arrive, 0)
        first, rows = CHUNKS[g]
        for t in range(first, first + rows, 16):
            pair = every[:, t : t + 16, :].astype(F32).reshape(NC, 2, 8, 128)
            for i in range(2):
                row = t // 8 + i
                if row == 7:
                    continue
                turned = pair[:, i].reshape(128, 128)
                x[row, :, 0:128] = (turned * gate[0]).astype(BF16)
                x[row, :, 128:256] = (turned * gate[1]).astype(BF16)
        if g == 0:
            y = dot(wz[...].reshape(128, 896), x[0:7].reshape(896, 256))
            for c in range(2):
                ob[c, 0:7] = y[64 * c : 64 * c + 56].reshape(7, 8, 256)
        else:
            w, n, lo = ((w1, 6, 8), (w2, 5, 20))[g - 1]
            flat = w[...].reshape(32 * n, 128 * n)
            plus = dot(flat, x[lo : lo + n].reshape(128 * n, 256))
            minus = dot(flat, x[lo + n : lo + 2 * n].reshape(128 * n, 256))
            for c in range(2):
                real, imag = 16 * n * c, 16 * n * c + 8 * n
                ob[c, lo - 1 : lo - 1 + n] = (
                    plus[real : real + 8 * n] - minus[imag : imag + 8 * n]
                ).reshape(n, 8, 256)
                ob[c, lo - 1 + n : lo - 1 + 2 * n] = (
                    minus[real : real + 8 * n] + plus[imag : imag + 8 * n]
                ).reshape(n, 8, 256)
    swap = remote(ob.at[other], orecv, o_send, o_recv, (space, sibling))
    swap.start()

    def turn_back(half, rows):
        for degree in range(7):
            width = 2 * degree + 1
            ahead = back = None
            for order in range(HEIGHT[degree]):
                at = OFFSET[degree] + order * width
                block = r3[half, at : at + width]
                line = rows(row_of(degree, order))
                one, two = block * line[:, :128], block * line[:, 128:]
                ahead = one if ahead is None else ahead + one
                back = two if back is None else back + two
            pf[half, degree * degree : (degree + 1) ** 2] = ahead
            pt[half, degree * degree : (degree + 1) ** 2] = back

    turn_back(core, lambda row: ob[core, row])
    swap.wait_recv()
    turn_back(other, lambda row: orecv[row])

    total = fcoef[...]
    for half in range(2):
        hi, lo = split(pf[half].reshape(392, 128))
        hot = nconst[3, :, 128 * half : 128 * half + 128]
        total = total + dot_nt(
            jnp.concatenate([hi, lo], axis=1), jnp.concatenate([hot, hot], axis=1)
        )
    hidden = total.reshape(49, 8, 128)
    lead = hidden[0]
    sigma = jax.nn.sigmoid(lead)
    energy = ewcol[0] * (lead * sigma)
    grads = [(ewcol[0] * (sigma * (1.0 + lead * (1.0 - sigma))))[None]]
    for degree in range(1, 7):
        block = hidden[degree * degree : (degree + 1) ** 2]
        square = 1.0 + jnp.sum(block * block, axis=0)
        energy = energy + ewcol[degree] * jnp.log(square)
        grads.append((ewcol[degree] * 2.0 / square) * block)
    hi, lo = split(jnp.concatenate(grads, axis=0).reshape(392, 128))
    hot = nconst[3]
    edge_grads = dot(
        jnp.concatenate([hi, lo], axis=1), jnp.concatenate([hot, hot], axis=0)
    )
    parts = []
    for half in range(2):
        block = edge_grads[:, 128 * half : 128 * half + 128].reshape(49, 8, 128)
        parts.append(jnp.sum(jnp.sum(block * pt[half], axis=0), axis=0, keepdims=True))
    parts.append(jnp.sum(energy, axis=0, keepdims=True))
    red[chan] = jnp.concatenate(parts + [jnp.zeros((5, 128), F32)], axis=0)

    def sums(d):
        to = lax.rem(chan + d, NC)
        return remote(red.at[chan], red.at[chan], r_send.at[d - 1], r_recv.at[d - 1], (space, to))

    def launch_sums(d, carry):
        sums(d).start()
        return carry

    def arrive_sums(d, carry):
        sums(d).wait_recv()
        return carry

    lax.fori_loop(1, NC, launch_sums, 0)
    lax.fori_loop(1, NC, arrive_sums, 0)
    summed = jnp.sum(red[...], axis=0)
    energy_out[...] = summed[2:3]
    pull = jnp.concatenate([summed[0:1], summed[1:2]], axis=1)
    push = jnp.concatenate([pull * u for u in unit] + [jnp.zeros((5, 256), F32)], axis=0)
    hi, lo = split(push)
    hilo = jnp.concatenate([hi.astype(F32), lo.astype(F32)], axis=0).astype(BF16)
    owed = []
    for side in range(2):
        part = dot_nt(hilo, nconst[1 + side])
        fsend[side] = part[0:8] + part[8:16]
    back = [
        remote(fsend.at[0], frecv.at[0], f_send.at[0], f_recv.at[0], (before, chan)),
        remote(fsend.at[1], frecv.at[1], f_send.at[1], f_recv.at[1], (after, chan)),
    ]
    for copy in back:
        copy.start()
    part = dot_nt(hilo, nconst[0]) - dot_nt(hilo, nconst[3])
    part = part[0:8] + part[8:16]
    for copy in back:
        copy.wait_recv()
    force_out[...] = (part + frecv[0] + frecv[1])[0:3]

    for copy in exchange + weights + [swap] + back:
        copy.wait_send()

    def drain(d, carry):
        for g in range(3):
            transfers(d, g).wait_send()
        sums(d).wait_send()
        return carry

    lax.fori_loop(1, NC, drain, 0)


def local(
    features, ghost_index, edge_src, edge_dst, edge_count, rotation, distance, edge_angle,
    radial_weight, conv_zero, conv_one, conv_two, energy_weight,
):
    vmem = pl.BlockSpec(memory_space=pltpu.VMEM)
    dma = pltpu.SemaphoreType.DMA
    energy, forces = pl.pallas_call(
        kernel,
        out_shape=(jax.ShapeDtypeStruct((1, 128), F32), jax.ShapeDtypeStruct((3, 128), F32)),
        in_specs=[vmem] * 13,
        out_specs=(vmem, vmem),
        scratch_shapes=[
            pltpu.VMEM((400, 128), BF16),
            pltpu.VMEM((8, 128), jnp.int32),
            pltpu.VMEM((2, 400, 128), BF16),
            pltpu.VMEM((2, 8, 128), jnp.int32),
            pltpu.VMEM((2, 64, 896), BF16),
            pltpu.VMEM((2, 96, 768), BF16),
            pltpu.VMEM((2, 80, 640), BF16),
            pltpu.VMEM((240, 256), F32),
            pltpu.VMEM((2, 235, 8, 128), F32),
            pltpu.VMEM((2, 49, 8, 128), F32),
            pltpu.VMEM((2, 30, 8, 128), F32),
            pltpu.VMEM((2, 240, 128), BF16),
            pltpu.VMEM((NC, 240, 128), BF16),
            pltpu.VMEM((2, 128, 128), F32),
            pltpu.VMEM((30, 128, 256), BF16),
            pltpu.VMEM((2, 29, 8, 256), F32),
            pltpu.VMEM((29, 8, 256), F32),
            pltpu.VMEM((2, 49, 8, 128), F32),
            pltpu.VMEM((2, 49, 8, 128), F32),
            pltpu.VMEM((392, 128), F32),
            pltpu.VMEM((4, 128, 256), BF16),
            pltpu.VMEM((7, 8, 128), F32),
            pltpu.VMEM((NC, 8, 128), F32),
            pltpu.VMEM((2, 8, 128), F32),
            pltpu.VMEM((2, 8, 128), F32),
            dma((4,)),
            dma((4,)),
            dma((3,)),
            dma((3,)),
            dma((NC - 1, 3)),
            dma((NC - 1, 3)),
            dma,
            dma,
            dma((NC - 1,)),
            dma((NC - 1,)),
            dma((2,)),
            dma((2,)),
        ],
        compiler_params=pltpu.CompilerParams(
            collective_id=0, has_side_effects=True, vmem_limit_bytes=48 * 1024 * 1024
        ),
        cost_estimate=pl.CostEstimate(flops=400_000_000, bytes_accessed=3_000_000, transcendentals=200_000),
    )(
        features,
        ghost_index,
        edge_src.reshape(1, 256),
        edge_dst.reshape(1, 256),
        edge_count.reshape(1, 1),
        rotation,
        distance.reshape(2, 128),
        edge_angle,
        radial_weight,
        conv_zero,
        conv_one,
        conv_two,
        energy_weight,
    )
    return (energy.reshape(128), forces)


def solution(mesh):
    in_specs = (
        P(None, "chan", "space"),
        P(None, "space"),
        P("space"),
        P("space"),
        P("space"),
        P(None, "space"),
        P("space"),
        P(None, "space"),
        P(),
        P(None, "chan", None),
        P(None, None, "chan", None),
        P(None, None, "chan", None),
        P(None, "chan"),
    )
    out_specs = (P("space"), P(None, "space"))
    return jax.shard_map(local, mesh=mesh, in_specs=in_specs, out_specs=out_specs, check_vma=False)
```

profile of v0, /device:TPU:1, one launch (start us, length us, event | category | flops | bytes accessed | tf_op | source)
XLA Modules:
  0.0 51.7 jit_solution(285435895315844479)
XLA Ops:
  0.6 0.0 copy-start.9
  0.6 0.0 copy-start.10
  1.3 0.0 copy-start.6
  1.3 0.0 copy-start.7
  1.3 0.0 copy-start.8
  1.3 0.0 copy-done.9
  1.4 0.0 copy-done.10
  1.4 0.6 %copy-done.6 = f32[7,8]{1,0:T(8,128)S(1)} copy-done((f32[7,8]{1,0:T(8,128)S(1)}, f32[7,8]{1,0:T(8,128)}, u32[]{:S(2)}) %copy-start.6) | copy-done | bytes 248
  2.0 0.0 copy-done.7
  2.0 0.0 copy-done.8
  2.0 0.0 copy-start
  2.0 0.9 %copy-done = bf16[2,6,8,768]{3,2,1,0:T(8,128)(2,1)S(1)} copy-done((bf16[2,6,8,768]{3,2,1,0:T(8,128)(2,1)S(1)}, bf16[2,6,8,768]{3,2,1,0:T(8,128)(2,1)}, u32[]{:S(2)}) %copy-start) | copy-done | bytes 147480
  2.9 0.0 copy-start.1
  2.9 0.9 %copy-done.1 = bf16[512,128]{1,0:T(8,128)(2,1)S(1)} copy-done((bf16[512,128]{1,0:T(8,128)(2,1)S(1)}, bf16[512,128]{1,0:T(8,128)(2,1)}, u32[]{:S(2)}) %copy-start.1) | copy-done | bytes 131096
  3.8 0.0 copy-start.2
  3.8 0.9 %copy-done.2 = bf16[235,256]{1,0:T(8,128)(2,1)S(1)} copy-done((bf16[235,256]{1,0:T(8,128)(2,1)S(1)}, bf16[235,256]{1,0:T(8,128)(2,1)}, u32[]{:S(2)}) %copy-start.2) | copy-done | bytes 120344
  4.7 0.0 copy-start.3
  4.8 0.9 %copy-done.3 = bf16[2,5,8,640]{3,2,1,0:T(8,128)(2,1)S(1)} copy-done((bf16[2,5,8,640]{3,2,1,0:T(8,128)(2,1)S(1)}, bf16[2,5,8,640]{3,2,1,0:T(8,128)(2,1)}, u32[]{:S(2)}) %copy-start.3) | copy-done | bytes 102424
  5.6 0.0 copy-start.4
  5.6 0.9 %copy-done.4 = bf16[49,8,128]{2,1,0:T(8,128)(2,1)S(1)} copy-done((bf16[49,8,128]{2,1,0:T(8,128)(2,1)S(1)}, bf16[49,8,128]{2,1,0:T(8,128)(2,1)}, u32[]{:S(2)}) %copy-start.4) | copy-done | bytes 100376
  6.5 0.0 copy-start.5
  6.5 0.9 %copy-done.5 = bf16[7,8,896]{2,1,0:T(8,128)(2,1)S(1)} copy-done((bf16[7,8,896]{2,1,0:T(8,128)(2,1)S(1)}, bf16[7,8,896]{2,1,0:T(8,128)(2,1)}, u32[]{:S(2)}) %copy-start.5) | copy-done | bytes 100376
  7.4 0.0 copy-start.11
  7.4 0.7 %copy-done.11 = f32[256]{0:T(256)S(1)} copy-done((f32[256]{0:T(256)S(1)}, f32[256]{0:T(256)}, u32[]{:S(2)}) %copy-start.11) | copy-done | bytes 1048
  8.1 42.5 %shard_map.140 = (f32[1,128]{1,0:T(1,128)S(1)}, f32[3,128]{1,0:T(4,128)S(1)}) custom-call(bf16[49,8,128]{2,1,0:T(8,128)(2,1)S(1)} %copy-done.4, s32[2,64]{1,0:T(2,128)S(1)} %copy-done.8, s32[1,256]{1,0:T(1,128)S(1)} %bitcast.6, s32[1,256]{1,0:T(1,128)S(1)} %bitcast.7, s32[1,1]{1,0:T(1,128)} %bitcast.5.count, bf16[235,256]{1,0:T(8,128)(2,1)S(1)} %copy-done.2, ...), custom_call_target="tpu_custom_call" | custom-call | flops 400000000 | bytes 3000000 | tf_op jit(solution)/shard_map/pallas_call | solution.py:332
  50.6 0.5 copy.18
  51.1 0.6 %copy.19 = f32[3,128]{1,0:T(4,128)} copy(f32[3,128]{1,0:T(4,128)S(1)} %get-tuple-element.9) | data formatting | bytes 3072
Async XLA Ops:
  0.6 0.7 %copy-start.9 = (s32[256]{0:T(256)S(1)}, s32[256]{0:T(256)}, u32[]{:S(2)}) copy-start(s32[256]{0:T(256)} %param.15) | copy-start | bytes 3076
  0.6 0.7 %copy-start.10 = (s32[256]{0:T(256)S(1)}, s32[256]{0:T(256)}, u32[]{:S(2)}) copy-start(s32[256]{0:T(256)} %param.16) | copy-start | bytes 3076
  1.3 0.7 %copy-start.6 = (f32[7,8]{1,0:T(8,128)S(1)}, f32[7,8]{1,0:T(8,128)}, u32[]{:S(2)}) copy-start(f32[7,8]{1,0:T(8,128)} %eweight.1) | copy-start | bytes 676
  1.3 0.7 %copy-start.7 = (f32[2,256]{1,0:T(2,128)S(1)}, f32[2,256]{1,0:T(2,128)}, u32[]{:S(2)}) copy-start(f32[2,256]{1,0:T(2,128)} %ang.1) | copy-start | bytes 6148
  1.3 0.7 %copy-start.8 = (s32[2,64]{1,0:T(2,128)S(1)}, s32[2,64]{1,0:T(2,128)}, u32[]{:S(2)}) copy-start(s32[2,64]{1,0:T(2,128)} %gidx.1) | copy-start | bytes 1540
  2.0 0.9 %copy-start = (bf16[2,6,8,768]{3,2,1,0:T(8,128)(2,1)S(1)}, bf16[2,6,8,768]{3,2,1,0:T(8,128)(2,1)}, u32[]{:S(2)}) copy-start(bf16[2,6,8,768]{3,2,1,0:T(8,128)(2,1)} %wone.1) | copy-start | bytes 442372
  2.9 0.9 %copy-start.1 = (bf16[512,128]{1,0:T(8,128)(2,1)S(1)}, bf16[512,128]{1,0:T(8,128)(2,1)}, u32[]{:S(2)}) copy-start(bf16[512,128]{1,0:T(8,128)(2,1)} %radial.1) | copy-start | bytes 393220
  3.8 0.9 %copy-start.2 = (bf16[235,256]{1,0:T(8,128)(2,1)S(1)}, bf16[235,256]{1,0:T(8,128)(2,1)}, u32[]{:S(2)}) copy-start(bf16[235,256]{1,0:T(8,128)(2,1)} %rot.1) | copy-start | bytes 360964
  4.7 0.9 %copy-start.3 = (bf16[2,5,8,640]{3,2,1,0:T(8,128)(2,1)S(1)}, bf16[2,5,8,640]{3,2,1,0:T(8,128)(2,1)}, u32[]{:S(2)}) copy-start(bf16[2,5,8,640]{3,2,1,0:T(8,128)(2,1)} %wtwo.1) | copy-start | bytes 307204
  5.6 0.9 %copy-start.4 = (bf16[49,8,128]{2,1,0:T(8,128)(2,1)S(1)}, bf16[49,8,128]{2,1,0:T(8,128)(2,1)}, u32[]{:S(2)}) copy-start(bf16[49,8,128]{2,1,0:T(8,128)(2,1)} %feat.1) | copy-start | bytes 301060
  6.5 0.9 %copy-start.5 = (bf16[7,8,896]{2,1,0:T(8,128)(2,1)S(1)}, bf16[7,8,896]{2,1,0:T(8,128)(2,1)}, u32[]{:S(2)}) copy-start(bf16[7,8,896]{2,1,0:T(8,128)(2,1)} %wzero.1) | copy-start | bytes 301060
  7.4 0.7 %copy-start.11 = (f32[256]{0:T(256)S(1)}, f32[256]{0:T(256)}, u32[]{:S(2)}) copy-start(f32[256]{0:T(256)} %param.19) | copy-start | bytes 3076
where the time goes:
time: 52 us; the launch traced here: 51.7 us
  Pallas kernels  42.5 us (82%)
  local copies, waits for them, and re-layouts  7.84 us (15%)
  between operations  1.37 us (3%)
    pallas_call x1, Pallas kernels, local(): pl.pallas_call(kernel, out_shape=(jax.ShapeDtypeStruct((1, 128), F32), ja...  42.5 us
    unnamed x26, local copies, waits for them, and re-layouts  7.84 us

commit v1 on v0

--- a/solution.py
+++ b/solution.py
@@ -14,6 +14,7 @@
 OFFSET = [sum(HEIGHT[m] * (2 * m + 1) for m in range(l)) for l in range(7)]
 FIRST = (0, 7, 13, 19, 24)
 LEAST = (0, 1, 1, 2, 2)
+FETCH_ORDER = (0, 1, 9, 10, 11, 5, 2, 3, 4, 6, 8, 12, 7)
 
 
 def row_of(degree, order):
@@ -37,13 +38,21 @@
     return hi, (x - hi.astype(F32)).astype(BF16)
 
 
-def kernel(
-    feat, gidx, esrc, edst, count, rot, dist, ang, radial, wzero, wone, wtwo, eweight,
-    energy_out, force_out,
-    mine, mine_g, ghost, ghost_g, wz, w1, w2, rf, r3, s3, t3, snd, every, gate, x, ob, orecv,
-    pf, pt, fcoef, nconst, ewcol, red, fsend, frecv,
-    g_send, g_recv, w_send, w_recv, a_send, a_recv, o_send, o_recv, r_send, r_recv, f_send, f_recv,
-):
+def kernel(*refs):
+    held = refs[:13]
+    energy_out, force_out = refs[13:15]
+    feat, gidx, esrc, edst, count, rot, dist, ang, radial, wzero, wone, wtwo, eweight = refs[15:28]
+    (
+        coef, base, shot, mine, mine_g, ghost, ghost_g, wz, w1, w2, rf, r3, s3, t3, snd, every, gate, x, ob, orecv,
+        pf, pt, fcoef, nconst, ewcol, red, fsend, frecv,
+        g_send, g_recv, w_send, w_recv, a_send, a_recv, o_send, o_recv, r_send, r_recv, f_send, f_recv, h_recv,
+    ) = refs[28:]
+    fetch = [
+        pltpu.make_async_copy(src, dst, h_recv.at[i])
+        for i, (src, dst) in enumerate(zip(held, refs[15:28]))
+    ]
+    for i in FETCH_ORDER:
+        fetch[i].start()
     space = lax.axis_index("space")
     chan = lax.axis_index("chan")
     n_space = lax.axis_size("space")
@@ -68,23 +77,35 @@
     pl.semaphore_signal(barrier, inc=1, device_id=(after, chan), device_id_type=MESH)
     pl.semaphore_signal(barrier, inc=1, device_id=(before, chan), device_id_type=MESH)
 
+    fetch[0].wait()
+    fetch[1].wait()
     own = feat[...].astype(F32).reshape(392, 128)
     fcoef[...] = own
-    mine[0:392, :] = own.astype(BF16)
-    mine[384:400, :] = jnp.concatenate([own[384:392], jnp.zeros((8, 128), F32)], axis=0).astype(BF16)
+    own = jnp.concatenate([own, jnp.zeros((24, 128), F32)], axis=0).astype(BF16)
+    coef[...] = own
+    lend_row = lax.broadcasted_iota(jnp.int32, (256, 256), 0)
+    lend_at = jnp.concatenate(
+        [gidx[0:1, :], gidx[0:1, :] + 128, gidx[1:2, :], gidx[1:2, :] + 128], axis=1
+    )
+    lend_hot = (lend_at == lend_row).astype(F32).astype(BF16)
+    lent = dot(jnp.concatenate([own[:208], own[208:]], axis=1), lend_hot).astype(BF16)
+    mine[0] = lent[:, :128]
+    mine[1] = lent[:, 128:]
     mine_g[...] = jnp.zeros((8, 128), jnp.int32)
     mine_g[0:2, 0:64] = gidx[...]
     pl.semaphore_wait(barrier, NC + 1)
 
     exchange = [
-        remote(mine, ghost.at[0], g_send.at[0], g_recv.at[0], (after, chan)),
-        remote(mine, ghost.at[1], g_send.at[1], g_recv.at[1], (before, chan)),
+        remote(mine.at[0], ghost.at[0], g_send.at[0], g_recv.at[0], (after, chan)),
+        remote(mine.at[1], ghost.at[1], g_send.at[1], g_recv.at[1], (before, chan)),
         remote(mine_g, ghost_g.at[0], g_send.at[2], g_recv.at[2], (after, chan)),
         remote(mine_g, ghost_g.at[1], g_send.at[3], g_recv.at[3], (before, chan)),
     ]
     for copy in exchange:
         copy.start()
 
+    for i in (9, 10, 11):
+        fetch[i].wait()
     wz[core] = jnp.concatenate(
         [wzero[...].astype(F32).reshape(56, 896), jnp.zeros((8, 896), F32)], axis=0
     ).astype(BF16)
@@ -97,6 +118,7 @@
     for copy in weights:
         copy.start()
 
+    fetch[5].wait()
     rf[0:235, :] = rot[...].astype(F32)
 
     def spread(i, carry):
@@ -109,15 +131,24 @@
 
     lax.fori_loop(0, 47, spread, 0)
 
+    for i in (2, 3, 4, 6, 7, 8, 12):
+        fetch[i].wait()
     atom_row = lax.broadcasted_iota(jnp.int32, (128, 256), 0)
     source = esrc[...]
     target_hot = (edst[...] == atom_row).astype(F32)
     source_hot = (source == atom_row).astype(F32)
     nconst[0] = source_hot.astype(BF16)
     nconst[3] = target_hot.astype(BF16)
-    base_coeffs = dot(mine[...], nconst[0])
-
-    live = (lax.broadcasted_iota(jnp.int32, (1, 128), 1) + core * 128 < count[...]).astype(F32)
+    base[...] = dot(coef[...], nconst[0])
+    slot_row = lax.broadcasted_iota(jnp.int32, (256, 256), 0)
+    slot_of = slot_row - 64 * (slot_row // 64) + 64 * (slot_row // 128)
+    upper = (slot_row // 64) % 2
+    for half in range(2):
+        shot[:, 256 * half : 256 * half + 256] = (
+            (source - 128 == jnp.where(upper == half, slot_of, -1000)).astype(F32).astype(BF16)
+        )
+
+    live = (lax.broadcasted_iota(jnp.int32, (1, 128), 1) + core * 128 < count[0]).astype(F32)
     center = 12.0 * lax.broadcasted_iota(jnp.int32, (512, 128), 0).astype(F32) / 511.0
     grid = dist[pl.ds(core, 1), :] - center
     basis = jnp.exp(-2.0 * grid * grid)
@@ -141,29 +172,56 @@
     polar, azimuth = ang[0:1, :], ang[1:2, :]
     unit = [jnp.sin(polar) * jnp.cos(azimuth), jnp.sin(polar) * jnp.sin(azimuth), jnp.cos(polar)]
 
-    slot_row = lax.broadcasted_iota(jnp.int32, (64, 256), 0)
-    atom_lane = lax.broadcasted_iota(jnp.int32, (128, 64), 0)
-    for copy in exchange:
+    for copy in exchange[:2]:
         copy.wait_recv()
-    coeffs = base_coeffs
-    for side in range(2):
-        slot_hot = (source - (128 + 64 * side) == slot_row).astype(F32).astype(BF16)
-        lent_hot = (ghost_g[side, side : side + 1, 0:64] == atom_lane).astype(F32).astype(BF16)
-        nconst[1 + side] = dot(lent_hot, slot_hot).astype(BF16)
-        coeffs = coeffs + dot(ghost[side], nconst[1 + side])
-    s3[0] = coeffs[0:392, :128].reshape(49, 8, 128)
-    s3[1] = coeffs[0:392, 128:].reshape(49, 8, 128)
-
-    def transfers(d, g):
-        first, rows = CHUNKS[g]
-        to = lax.rem(chan + d, NC)
+    lent = dot(jnp.concatenate([ghost[0], ghost[1]], axis=1), shot[...])
+    for half in range(2):
+        at = 128 * half
+        s3[half, 0:26] = (base[0:208, at : at + 128] + lent[:, at : at + 128]).reshape(26, 8, 128)
+        s3[half, 26:49] = (
+            base[208:392, at : at + 128] + lent[0:184, 256 + at : 384 + at]
+        ).reshape(23, 8, 128)
+
+    along, deep = lax.div(chan, 4), lax.rem(lax.div(chan, 2), 2)
+
+    def peer(dy, dz, c):
+        return lax.rem(along + dy, 4) * 4 + lax.rem(deep + dz, 2) * 2 + c
+
+    def piece_of(ref, g, first, count):
+        start, rows = CHUNKS[g]
+        return ref.at[pl.ds(first, count), pl.ds(start, rows)]
+
+    def own_sends(g):
+        plans = [(sibling, other, 0)]
+        for c in range(2):
+            plans.append((peer(0, 1, c), c, 1 + core))
+            plans.append((peer(1, 0, c), c, 3 + core))
+            plans.append((peer(3, 0, c), c, 5 + core))
+        return [
+            remote(piece_of(snd, g, half, 1), piece_of(every, g, chan, 1), a_send.at[i, g], a_recv.at[kind, g], (space, to))
+            for i, (to, half, kind) in enumerate(plans)
+        ]
+
+    def relay(g, slot, kind, first, count, to):
         return remote(
-            snd.at[lax.rem(to, 2), pl.ds(first, rows)],
-            every.at[chan, pl.ds(first, rows)],
-            a_send.at[d - 1, g],
-            a_recv.at[d - 1, g],
-            (space, to),
+            piece_of(every, g, first, count), piece_of(every, g, first, count), a_send.at[slot, g], a_recv.at[kind, g], (space, to)
         )
+
+    ahead, behind, across = peer(1, 0, core), peer(3, 0, core), peer(0, 1, core)
+    paths = [
+        (peer(0, 1, 0), 2, ahead),
+        (peer(0, 1, 0), 2, behind),
+        (peer(3, 0, 0), 1, ahead),
+        (peer(1, 0, 1), 1, behind),
+        (peer(2, 0, 0), 1, across),
+        (peer(2, 0, 1), 1, across),
+    ]
+
+    def passed(g, i):
+        return relay(g, 7 + i, 7 + i, *paths[i])
+
+    def landed(g, kind, first, count):
+        relay(g, 0, kind, first, count, sibling).wait_recv()
 
     t3[:, 7] = jnp.zeros((2, 8, 128), F32)
     for g in range(3):
@@ -183,21 +241,42 @@
             )
         every[chan, first : first + rows] = snd[core, first : first + rows]
 
-        def launch(d, carry):
-            transfers(d, g).start()
-            return carry
-
-        lax.fori_loop(1, NC, launch, 0)
-
+        for copy in own_sends(g):
+            copy.start()
+
+    for g in range(3):
+        for c in range(2):
+            landed(g, 1 + c, peer(0, 1, c), 1)
+        passed(g, 0).start()
+        passed(g, 1).start()
+        landed(g, 3, peer(3, 0, 0), 1)
+        passed(g, 2).start()
+        landed(g, 6, peer(1, 0, 1), 1)
+        passed(g, 3).start()
+    for g in range(3):
+        landed(g, 9, peer(2, 0, 0), 1)
+        passed(g, 4).start()
+        landed(g, 10, peer(2, 0, 1), 1)
+        passed(g, 5).start()
+
+    for copy in exchange[2:]:
+        copy.wait_recv()
+    slot_row = lax.broadcasted_iota(jnp.int32, (64, 256), 0)
+    atom_lane = lax.broadcasted_iota(jnp.int32, (128, 64), 0)
+    for side in range(2):
+        slot_hot = (source - (128 + 64 * side) == slot_row).astype(F32).astype(BF16)
+        lent_hot = (ghost_g[side, side : side + 1, 0:64] == atom_lane).astype(F32).astype(BF16)
+        nconst[1 + side] = dot(lent_hot, slot_hot).astype(BF16)
     for copy in weights:
         copy.wait_recv()
     for g in range(3):
-
-        def arrive(d, carry):
-            transfers(d, g).wait_recv()
-            return carry
-
-        lax.fori_loop(1, NC, arrive, 0)
+        landed(g, 0, sibling, 1)
+        landed(g, 4, peer(3, 0, 1), 1)
+        landed(g, 5, peer(1, 0, 0), 1)
+        landed(g, 7, peer(3, 1, 0), 2)
+        landed(g, 8, peer(1, 1, 0), 2)
+        landed(g, 11, peer(2, 1, 0), 1)
+        landed(g, 12, peer(2, 1, 1), 1)
         first, rows = CHUNKS[g]
         for t in range(first, first + rows, 16):
             pair = every[:, t : t + 16, :].astype(F32).reshape(NC, 2, 8, 128)
@@ -295,7 +374,6 @@
     push = jnp.concatenate([pull * u for u in unit] + [jnp.zeros((5, 256), F32)], axis=0)
     hi, lo = split(push)
     hilo = jnp.concatenate([hi.astype(F32), lo.astype(F32)], axis=0).astype(BF16)
-    owed = []
     for side in range(2):
         part = dot_nt(hilo, nconst[1 + side])
         fsend[side] = part[0:8] + part[8:16]
@@ -311,12 +389,13 @@
         copy.wait_recv()
     force_out[...] = (part + frecv[0] + frecv[1])[0:3]
 
-    for copy in exchange + weights + [swap] + back:
+    sent = exchange + weights + [swap] + back
+    for g in range(3):
+        sent = sent + own_sends(g) + [passed(g, i) for i in range(6)]
+    for copy in sent:
         copy.wait_send()
 
     def drain(d, carry):
-        for g in range(3):
-            transfers(d, g).wait_send()
         sums(d).wait_send()
         return carry
 
@@ -328,16 +407,35 @@
     radial_weight, conv_zero, conv_one, conv_two, energy_weight,
 ):
     vmem = pl.BlockSpec(memory_space=pltpu.VMEM)
+    arrays = (
+        features,
+        ghost_index,
+        edge_src.reshape(1, 256),
+        edge_dst.reshape(1, 256),
+        edge_count,
+        rotation,
+        distance.reshape(2, 128),
+        edge_angle,
+        radial_weight,
+        conv_zero,
+        conv_one,
+        conv_two,
+        energy_weight,
+    )
     dma = pltpu.SemaphoreType.DMA
     energy, forces = pl.pallas_call(
         kernel,
         out_shape=(jax.ShapeDtypeStruct((1, 128), F32), jax.ShapeDtypeStruct((3, 128), F32)),
-        in_specs=[vmem] * 13,
+        in_specs=[pl.BlockSpec(memory_space=pl.ANY)] * 13,
         out_specs=(vmem, vmem),
-        scratch_shapes=[
-            pltpu.VMEM((400, 128), BF16),
+        scratch_shapes=[(pltpu.SMEM if a.shape == (1,) else pltpu.VMEM)(a.shape, a.dtype) for a in arrays]
+        + [
+            pltpu.VMEM((416, 128), BF16),
+            pltpu.VMEM((416, 256), F32),
+            pltpu.VMEM((256, 512), BF16),
+            pltpu.VMEM((2, 208, 128), BF16),
             pltpu.VMEM((8, 128), jnp.int32),
-            pltpu.VMEM((2, 400, 128), BF16),
+            pltpu.VMEM((2, 208, 128), BF16),
             pltpu.VMEM((2, 8, 128), jnp.int32),
             pltpu.VMEM((2, 64, 896), BF16),
             pltpu.VMEM((2, 96, 768), BF16),
@@ -364,34 +462,21 @@
             dma((4,)),
             dma((3,)),
             dma((3,)),
-            dma((NC - 1, 3)),
-            dma((NC - 1, 3)),
+            dma((13, 3)),
+            dma((13, 3)),
             dma,
             dma,
             dma((NC - 1,)),
             dma((NC - 1,)),
             dma((2,)),
             dma((2,)),
+            dma((13,)),
         ],
         compiler_params=pltpu.CompilerParams(
-            collective_id=0, has_side_effects=True, vmem_limit_bytes=48 * 1024 * 1024
+            collective_id=0, has_side_effects=True, vmem_limit_bytes=60 * 1024 * 1024
         ),
         cost_estimate=pl.CostEstimate(flops=400_000_000, bytes_accessed=3_000_000, transcendentals=200_000),
-    )(
-        features,
-        ghost_index,
-        edge_src.reshape(1, 256),
-        edge_dst.reshape(1, 256),
-        edge_count.reshape(1, 1),
-        rotation,
-        distance.reshape(2, 128),
-        edge_angle,
-        radial_weight,
-        conv_zero,
-        conv_one,
-        conv_two,
-        energy_weight,
-    )
+    )(*arrays)
     return (energy.reshape(128), forces)
 
 

time: 52 us -> 44.2 us (0.85)
  local copies, waits for them, and re-layouts: 7.84 us -> 1.71 us
  Pallas kernels: 42.5 us -> 41 us
    unnamed x26 -> x6, local copies, waits for them, and re-layouts: 7.84 us -> 1.71 us
    pallas_call x1, Pallas kernels: 42.5 us -> 41 us  [local(): pl.pallas_call(kernel, out_shape=(jax.ShapeDtypeStruct((1, 128), F32), ja...]
where the time goes in v1:
time: 44.2 us; the launch traced here: 44 us
  Pallas kernels  41 us (93%)
  local copies, waits for them, and re-layouts  1.71 us (4%)
  between operations  1.31 us (3%)
    pallas_call x1, Pallas kernels, local(): pl.pallas_call(kernel, out_shape=(jax.ShapeDtypeStruct((1, 128), F32), ja...  41 us
    unnamed x6, local copies, waits for them, and re-layouts  1.71 us

profile of v1, /device:TPU:1, one launch (start us, length us, event | category | flops | bytes accessed | tf_op | source)
XLA Modules:
  0.0 44.0 jit_solution(9970241145872082676)
XLA Ops:
  1.3 41.0 %shard_map.140 = (f32[1,128]{1,0:T(1,128)}, f32[3,128]{1,0:T(4,128)}) custom-call(bf16[49,8,128]{2,1,0:T(8,128)(2,1)} %refs_0_.1, s32[2,64]{1,0:T(2,128)} %refs_1_.1, s32[1,256]{1,0:T(1,128)} %bitcast.4, s32[1,256]{1,0:T(1,128)} %bitcast.5, s32[1]{0:T(128)S(6)} %copy.17.refs_4_, bf16[235,256]{1,0:T(8,128)(2,1)} %refs_5_.1, f32[2,128]{1,0:T(2,128)} %bitcast.6, ...), custom_call_target="tpu_custom_call" | custom-call | flops 400000000 | bytes 3000000 | tf_op jit(solution)/shard_map/pallas_call | solution.py:426
  42.3 0.0 copy-start.1
  42.3 0.0 copy-start
  42.3 0.6 %copy-done.1 = f32[1,128]{1,0:T(1,128)S(1)} copy-done((f32[1,128]{1,0:T(1,128)S(1)}, f32[1,128]{1,0:T(1,128)}, u32[]{:S(2)}) %copy-start.1) | copy-done | bytes 536
  43.0 0.5 %copy.18 = f32[128]{0:T(128)} copy(f32[128]{0:T(128)S(1)} %bitcast.7) | data formatting | bytes 1024
  43.5 0.0 copy-done
  43.5 0.6 %copy.19 = f32[3,128]{1,0:T(4,128)} copy(f32[3,128]{1,0:T(4,128)S(1)} %copy-done) | data formatting | bytes 3072
Async XLA Ops:
  42.3 0.6 %copy-start.1 = (f32[1,128]{1,0:T(1,128)S(1)}, f32[1,128]{1,0:T(1,128)}, u32[]{:S(2)}) copy-start(f32[1,128]{1,0:T(1,128)} %get-tuple-element.4) | copy-start | bytes 1540
  42.3 1.1 %copy-start = (f32[3,128]{1,0:T(4,128)S(1)}, f32[3,128]{1,0:T(4,128)}, u32[]{:S(2)}) copy-start(f32[3,128]{1,0:T(4,128)} %get-tuple-element.9) | copy-start | bytes 4612

commit v2 on v1

--- a/solution.py
+++ b/solution.py
@@ -14,7 +14,7 @@
 OFFSET = [sum(HEIGHT[m] * (2 * m + 1) for m in range(l)) for l in range(7)]
 FIRST = (0, 7, 13, 19, 24)
 LEAST = (0, 1, 1, 2, 2)
-FETCH_ORDER = (0, 1, 9, 10, 11, 5, 2, 3, 4, 6, 8, 12, 7)
+FETCH_ORDER = (9, 10, 11, 5, 2, 3, 4, 6, 8, 12, 7)
 
 
 def row_of(degree, order):
@@ -44,15 +44,15 @@
     feat, gidx, esrc, edst, count, rot, dist, ang, radial, wzero, wone, wtwo, eweight = refs[15:28]
     (
         coef, base, shot, mine, mine_g, ghost, ghost_g, wz, w1, w2, rf, r3, s3, t3, snd, every, gate, x, ob, orecv,
-        pf, pt, fcoef, nconst, ewcol, red, fsend, frecv,
+        pf, pt, fcoef, nconst, pushes, ewcol, red, fsend, frecv,
         g_send, g_recv, w_send, w_recv, a_send, a_recv, o_send, o_recv, r_send, r_recv, f_send, f_recv, h_recv,
     ) = refs[28:]
     fetch = [
         pltpu.make_async_copy(src, dst, h_recv.at[i])
         for i, (src, dst) in enumerate(zip(held, refs[15:28]))
     ]
-    for i in FETCH_ORDER:
-        fetch[i].start()
+    fetch[0].start()
+    fetch[1].start()
     space = lax.axis_index("space")
     chan = lax.axis_index("chan")
     n_space = lax.axis_size("space")
@@ -73,9 +73,11 @@
         pl.semaphore_signal(barrier, inc=1, device_id=(space, lax.rem(chan + d, NC)), device_id_type=MESH)
         return carry
 
-    lax.fori_loop(1, NC, greet, 0)
     pl.semaphore_signal(barrier, inc=1, device_id=(after, chan), device_id_type=MESH)
     pl.semaphore_signal(barrier, inc=1, device_id=(before, chan), device_id_type=MESH)
+    lax.fori_loop(1, NC, greet, 0)
+    for i in FETCH_ORDER:
+        fetch[i].start()
 
     fetch[0].wait()
     fetch[1].wait()
@@ -97,10 +99,12 @@
 
     exchange = [
         remote(mine.at[0], ghost.at[0], g_send.at[0], g_recv.at[0], (after, chan)),
-        remote(mine.at[1], ghost.at[1], g_send.at[1], g_recv.at[1], (before, chan)),
-        remote(mine_g, ghost_g.at[0], g_send.at[2], g_recv.at[2], (after, chan)),
-        remote(mine_g, ghost_g.at[1], g_send.at[3], g_recv.at[3], (before, chan)),
+        remote(mine.at[1], ghost.at[1], g_send.at[0], g_recv.at[0], (before, chan)),
+        remote(mine_g, ghost_g.at[0], g_send.at[1], g_recv.at[1], (after, chan)),
+        remote(mine_g, ghost_g.at[1], g_send.at[1], g_recv.at[1], (before, chan)),
     ]
+    both_ghosts = remote(ghost, ghost, g_send.at[0], g_recv.at[0], (after, chan))
+    both_tables = remote(ghost_g, ghost_g, g_send.at[1], g_recv.at[1], (after, chan))
     for copy in exchange:
         copy.start()
 
@@ -138,7 +142,7 @@
     target_hot = (edst[...] == atom_row).astype(F32)
     source_hot = (source == atom_row).astype(F32)
     nconst[0] = source_hot.astype(BF16)
-    nconst[3] = target_hot.astype(BF16)
+    nconst[1] = target_hot.astype(BF16)
     base[...] = dot(coef[...], nconst[0])
     slot_row = lax.broadcasted_iota(jnp.int32, (256, 256), 0)
     slot_of = slot_row - 64 * (slot_row // 64) + 64 * (slot_row // 128)
@@ -172,8 +176,7 @@
     polar, azimuth = ang[0:1, :], ang[1:2, :]
     unit = [jnp.sin(polar) * jnp.cos(azimuth), jnp.sin(polar) * jnp.sin(azimuth), jnp.cos(polar)]
 
-    for copy in exchange[:2]:
-        copy.wait_recv()
+    both_ghosts.wait_recv()
     lent = dot(jnp.concatenate([ghost[0], ghost[1]], axis=1), shot[...])
     for half in range(2):
         at = 128 * half
@@ -191,37 +194,34 @@
         start, rows = CHUNKS[g]
         return ref.at[pl.ds(first, count), pl.ds(start, rows)]
 
+    def blocks(g, src, dst, source, first, count, kind, to):
+        return remote(
+            piece_of(src, g, source, count), piece_of(dst, g, first, count), a_send, a_recv.at[kind, g], (space, to)
+        )
+
     def own_sends(g):
         plans = [(sibling, other, 0)]
         for c in range(2):
-            plans.append((peer(0, 1, c), c, 1 + core))
-            plans.append((peer(1, 0, c), c, 3 + core))
-            plans.append((peer(3, 0, c), c, 5 + core))
-        return [
-            remote(piece_of(snd, g, half, 1), piece_of(every, g, chan, 1), a_send.at[i, g], a_recv.at[kind, g], (space, to))
-            for i, (to, half, kind) in enumerate(plans)
-        ]
-
-    def relay(g, slot, kind, first, count, to):
-        return remote(
-            piece_of(every, g, first, count), piece_of(every, g, first, count), a_send.at[slot, g], a_recv.at[kind, g], (space, to)
-        )
+            plans.append((peer(0, 1, c), c, 1))
+        for c in range(2):
+            plans.append((peer(2, 0, c), c, 2))
+            plans.append((peer(1, 0, c), c, 0))
+            plans.append((peer(3, 0, c), c, 0))
+        return [blocks(g, snd, every, half, chan, 1, kind, to) for to, half, kind in plans]
 
     ahead, behind, across = peer(1, 0, core), peer(3, 0, core), peer(0, 1, core)
     paths = [
-        (peer(0, 1, 0), 2, ahead),
-        (peer(0, 1, 0), 2, behind),
-        (peer(3, 0, 0), 1, ahead),
-        (peer(1, 0, 1), 1, behind),
-        (peer(2, 0, 0), 1, across),
-        (peer(2, 0, 1), 1, across),
+        (peer(0, 1, 0), 2, 0, ahead),
+        (peer(0, 1, 0), 2, 0, behind),
+        (peer(2, 0, 0), 2, 0, across),
     ]
 
     def passed(g, i):
-        return relay(g, 7 + i, 7 + i, *paths[i])
-
-    def landed(g, kind, first, count):
-        relay(g, 0, kind, first, count, sibling).wait_recv()
+        first, count, kind, to = paths[i]
+        return blocks(g, every, every, first, first, count, kind, to)
+
+    def landed(g, kind, count):
+        blocks(g, every, every, 0, 0, count, kind, sibling).wait_recv()
 
     t3[:, 7] = jnp.zeros((2, 8, 128), F32)
     for g in range(3):
@@ -245,38 +245,24 @@
             copy.start()
 
     for g in range(3):
-        for c in range(2):
-            landed(g, 1 + c, peer(0, 1, c), 1)
+        landed(g, 1, 2)
         passed(g, 0).start()
         passed(g, 1).start()
-        landed(g, 3, peer(3, 0, 0), 1)
+        landed(g, 2, 2)
         passed(g, 2).start()
-        landed(g, 6, peer(1, 0, 1), 1)
-        passed(g, 3).start()
-    for g in range(3):
-        landed(g, 9, peer(2, 0, 0), 1)
-        passed(g, 4).start()
-        landed(g, 10, peer(2, 0, 1), 1)
-        passed(g, 5).start()
-
-    for copy in exchange[2:]:
-        copy.wait_recv()
+
+    both_tables.wait_recv()
     slot_row = lax.broadcasted_iota(jnp.int32, (64, 256), 0)
     atom_lane = lax.broadcasted_iota(jnp.int32, (128, 64), 0)
     for side in range(2):
         slot_hot = (source - (128 + 64 * side) == slot_row).astype(F32).astype(BF16)
         lent_hot = (ghost_g[side, side : side + 1, 0:64] == atom_lane).astype(F32).astype(BF16)
-        nconst[1 + side] = dot(lent_hot, slot_hot).astype(BF16)
+        pushes[:, 128 * side : 128 * side + 128] = dot(lent_hot, slot_hot).T.astype(BF16)
+    pushes[:, 256:384] = (nconst[0].astype(F32) - nconst[1].astype(F32)).T.astype(BF16)
     for copy in weights:
         copy.wait_recv()
     for g in range(3):
-        landed(g, 0, sibling, 1)
-        landed(g, 4, peer(3, 0, 1), 1)
-        landed(g, 5, peer(1, 0, 0), 1)
-        landed(g, 7, peer(3, 1, 0), 2)
-        landed(g, 8, peer(1, 1, 0), 2)
-        landed(g, 11, peer(2, 1, 0), 1)
-        landed(g, 12, peer(2, 1, 1), 1)
+        landed(g, 0, 11)
         first, rows = CHUNKS[g]
         for t in range(first, first + rows, 16):
             pair = every[:, t : t + 16, :].astype(F32).reshape(NC, 2, 8, 128)
@@ -304,8 +290,10 @@
                 ob[c, lo - 1 + n : lo - 1 + 2 * n] = (
                     minus[real : real + 8 * n] + plus[imag : imag + 8 * n]
                 ).reshape(n, 8, 256)
+        low, high = ((0, 7), (7, 19), (19, 29))[g]
+        rows = pl.ds(low, high - low)
+        remote(ob.at[other, rows], orecv.at[rows], o_send, o_recv, (space, sibling)).start()
     swap = remote(ob.at[other], orecv, o_send, o_recv, (space, sibling))
-    swap.start()
 
     def turn_back(half, rows):
         for degree in range(7):
@@ -328,7 +316,7 @@
     total = fcoef[...]
     for half in range(2):
         hi, lo = split(pf[half].reshape(392, 128))
-        hot = nconst[3, :, 128 * half : 128 * half + 128]
+        hot = nconst[1, :, 128 * half : 128 * half + 128]
         total = total + dot_nt(
             jnp.concatenate([hi, lo], axis=1), jnp.concatenate([hot, hot], axis=1)
         )
@@ -343,7 +331,7 @@
         energy = energy + ewcol[degree] * jnp.log(square)
         grads.append((ewcol[degree] * 2.0 / square) * block)
     hi, lo = split(jnp.concatenate(grads, axis=0).reshape(392, 128))
-    hot = nconst[3]
+    hot = nconst[1]
     edge_grads = dot(
         jnp.concatenate([hi, lo], axis=1), jnp.concatenate([hot, hot], axis=0)
     )
@@ -356,50 +344,43 @@
 
     def sums(d):
         to = lax.rem(chan + d, NC)
-        return remote(red.at[chan], red.at[chan], r_send.at[d - 1], r_recv.at[d - 1], (space, to))
+        return remote(red.at[chan], red.at[chan], r_send, r_recv, (space, to))
 
     def launch_sums(d, carry):
         sums(d).start()
         return carry
 
-    def arrive_sums(d, carry):
-        sums(d).wait_recv()
-        return carry
-
+    all_sums = remote(red.at[pl.ds(0, NC - 1)], red.at[pl.ds(0, NC - 1)], r_send, r_recv, (space, sibling))
     lax.fori_loop(1, NC, launch_sums, 0)
-    lax.fori_loop(1, NC, arrive_sums, 0)
+    both_ghosts.wait_send()
+    both_tables.wait_send()
+    for copy in weights + [swap]:
+        copy.wait_send()
+    whole = every.at[pl.ds(0, NC - 1)]
+    remote(whole, whole, a_send, a_recv.at[0, 0], (space, sibling)).wait_send()
+    all_sums.wait_recv()
     summed = jnp.sum(red[...], axis=0)
     energy_out[...] = summed[2:3]
     pull = jnp.concatenate([summed[0:1], summed[1:2]], axis=1)
     push = jnp.concatenate([pull * u for u in unit] + [jnp.zeros((5, 256), F32)], axis=0)
     hi, lo = split(push)
     hilo = jnp.concatenate([hi.astype(F32), lo.astype(F32)], axis=0).astype(BF16)
-    for side in range(2):
-        part = dot_nt(hilo, nconst[1 + side])
-        fsend[side] = part[0:8] + part[8:16]
+    part = dot(hilo, pushes[...])
+    part = part[0:8] + part[8:16]
+    fsend[0] = part[:, 0:128]
+    fsend[1] = part[:, 128:256]
     back = [
-        remote(fsend.at[0], frecv.at[0], f_send.at[0], f_recv.at[0], (before, chan)),
-        remote(fsend.at[1], frecv.at[1], f_send.at[1], f_recv.at[1], (after, chan)),
+        remote(fsend.at[0], frecv.at[0], f_send, f_recv, (before, chan)),
+        remote(fsend.at[1], frecv.at[1], f_send, f_recv, (after, chan)),
     ]
     for copy in back:
         copy.start()
-    part = dot_nt(hilo, nconst[0]) - dot_nt(hilo, nconst[3])
-    part = part[0:8] + part[8:16]
-    for copy in back:
-        copy.wait_recv()
-    force_out[...] = (part + frecv[0] + frecv[1])[0:3]
-
-    sent = exchange + weights + [swap] + back
-    for g in range(3):
-        sent = sent + own_sends(g) + [passed(g, i) for i in range(6)]
-    for copy in sent:
-        copy.wait_send()
-
-    def drain(d, carry):
-        sums(d).wait_send()
-        return carry
-
-    lax.fori_loop(1, NC, drain, 0)
+    both_back = remote(fsend, frecv, f_send, f_recv, (before, chan))
+    all_sums.wait_send()
+    both_back.wait_recv()
+    force_out[...] = (part[:, 256:384] + frecv[0] + frecv[1])[0:3]
+
+    both_back.wait_send()
 
 
 def local(
@@ -453,23 +434,24 @@
             pltpu.VMEM((2, 49, 8, 128), F32),
             pltpu.VMEM((2, 49, 8, 128), F32),
             pltpu.VMEM((392, 128), F32),
-            pltpu.VMEM((4, 128, 256), BF16),
+            pltpu.VMEM((2, 128, 256), BF16),
+            pltpu.VMEM((256, 384), BF16),
             pltpu.VMEM((7, 8, 128), F32),
             pltpu.VMEM((NC, 8, 128), F32),
             pltpu.VMEM((2, 8, 128), F32),
             pltpu.VMEM((2, 8, 128), F32),
-            dma((4,)),
-            dma((4,)),
+            dma((2,)),
+            dma((2,)),
             dma((3,)),
             dma((3,)),
-            dma((13, 3)),
-            dma((13, 3)),
-            dma,
-            dma,
-            dma((NC - 1,)),
-            dma((NC - 1,)),
-            dma((2,)),
-            dma((2,)),
+            dma,
+            dma((3, 3)),
+            dma,
+            dma,
+            dma,
+            dma,
+            dma,
+            dma,
             dma((13,)),
         ],
         compiler_params=pltpu.CompilerParams(

time: 44.2 us -> 40.4 us (0.914)
  Pallas kernels: 41 us -> 37.2 us
    pallas_call x1, Pallas kernels: 41 us -> 37.2 us  [local(): pl.pallas_call(kernel, out_shape=(jax.ShapeDtypeStruct((1, 128), F32), ja...]
where the time goes in v2:
time: 40.4 us; the launch traced here: 40.2 us
  Pallas kernels  37.2 us (92%)
  local copies, waits for them, and re-layouts  1.71 us (4%)
  between operations  1.31 us (3%)
    pallas_call x1, Pallas kernels, local(): pl.pallas_call(kernel, out_shape=(jax.ShapeDtypeStruct((1, 128), F32), ja...  37.2 us
    unnamed x6, local copies, waits for them, and re-layouts  1.71 us

profile of v2, /device:TPU:1, one launch (start us, length us, event | category | flops | bytes accessed | tf_op | source)
XLA Modules:
  0.0 40.2 jit_solution(15517238015599817753)
XLA Ops:
  1.3 37.2 %shard_map.140 = (f32[1,128]{1,0:T(1,128)}, f32[3,128]{1,0:T(4,128)}) custom-call(bf16[49,8,128]{2,1,0:T(8,128)(2,1)} %refs_0_.1, s32[2,64]{1,0:T(2,128)} %refs_1_.1, s32[1,256]{1,0:T(1,128)} %bitcast.4, s32[1,256]{1,0:T(1,128)} %bitcast.5, s32[1]{0:T(128)S(6)} %copy.17.refs_4_, bf16[235,256]{1,0:T(8,128)(2,1)} %refs_5_.1, f32[2,128]{1,0:T(2,128)} %bitcast.6, ...), custom_call_target="tpu_custom_call" | custom-call | flops 400000000 | bytes 3000000 | tf_op jit(solution)/shard_map/pallas_call | solution.py:407
  38.5 0.0 copy-start.1
  38.5 0.0 copy-start
  38.5 0.6 %copy-done.1 = f32[1,128]{1,0:T(1,128)S(1)} copy-done((f32[1,128]{1,0:T(1,128)S(1)}, f32[1,128]{1,0:T(1,128)}, u32[]{:S(2)}) %copy-start.1) | copy-done | bytes 536
  39.1 0.5 %copy.18 = f32[128]{0:T(128)} copy(f32[128]{0:T(128)S(1)} %bitcast.7) | data formatting | bytes 1024
  39.6 0.0 copy-done
  39.7 0.6 %copy.19 = f32[3,128]{1,0:T(4,128)} copy(f32[3,128]{1,0:T(4,128)S(1)} %copy-done) | data formatting | bytes 3072
Async XLA Ops:
  38.5 0.6 %copy-start.1 = (f32[1,128]{1,0:T(1,128)S(1)}, f32[1,128]{1,0:T(1,128)}, u32[]{:S(2)}) copy-start(f32[1,128]{1,0:T(1,128)} %get-tuple-element.4) | copy-start | bytes 1540
  38.5 1.1 %copy-start = (f32[3,128]{1,0:T(4,128)S(1)}, f32[3,128]{1,0:T(4,128)}, u32[]{:S(2)}) copy-start(f32[3,128]{1,0:T(4,128)} %get-tuple-element.9) | copy-start | bytes 4612

commit v3 on v2

--- a/solution.py
+++ b/solution.py
@@ -44,7 +44,7 @@
     feat, gidx, esrc, edst, count, rot, dist, ang, radial, wzero, wone, wtwo, eweight = refs[15:28]
     (
         coef, base, shot, mine, mine_g, ghost, ghost_g, wz, w1, w2, rf, r3, s3, t3, snd, every, gate, x, ob, orecv,
-        pf, pt, fcoef, nconst, pushes, ewcol, red, fsend, frecv,
+        pf, pt, fcoef, nconst, pushes, ewcol, red, fsend, frecv, fsum,
         g_send, g_recv, w_send, w_recv, a_send, a_recv, o_send, o_recv, r_send, r_recv, f_send, f_recv, h_recv,
     ) = refs[28:]
     fetch = [
@@ -67,15 +67,25 @@
             src_ref=src, dst_ref=dst, send_sem=send, recv_sem=recv, device_id=where, device_id_type=MESH
         )
 
+    along, deep = lax.div(chan, 4), lax.rem(lax.div(chan, 2), 2)
+
+    def peer(dy, dz, c):
+        return lax.rem(along + dy, 4) * 4 + lax.rem(deep + dz, 2) * 2 + c
+
+    chip = lax.div(chan, 2)
     barrier = pltpu.get_barrier_semaphore()
 
-    def greet(d, carry):
-        pl.semaphore_signal(barrier, inc=1, device_id=(space, lax.rem(chan + d, NC)), device_id_type=MESH)
-        return carry
-
-    pl.semaphore_signal(barrier, inc=1, device_id=(after, chan), device_id_type=MESH)
-    pl.semaphore_signal(barrier, inc=1, device_id=(before, chan), device_id_type=MESH)
-    lax.fori_loop(1, NC, greet, 0)
+    def greet(where):
+        pl.semaphore_signal(barrier, inc=1, device_id=where, device_id_type=MESH)
+
+    greet((after, chan))
+    greet((before, chan))
+    greet((space, sibling))
+    for c in range(2):
+        for dy, dz in ((0, 1), (1, 0), (3, 0), (2, 0)):
+            greet((space, peer(dy, dz, c)))
+    for dy in range(1, 4):
+        greet((space, peer(dy, 1, core)))
     for i in FETCH_ORDER:
         fetch[i].start()
 
@@ -95,7 +105,7 @@
     mine[1] = lent[:, 128:]
     mine_g[...] = jnp.zeros((8, 128), jnp.int32)
     mine_g[0:2, 0:64] = gidx[...]
-    pl.semaphore_wait(barrier, NC + 1)
+    pl.semaphore_wait(barrier, 14)
 
     exchange = [
         remote(mine.at[0], ghost.at[0], g_send.at[0], g_recv.at[0], (after, chan)),
@@ -185,11 +195,6 @@
             base[208:392, at : at + 128] + lent[0:184, 256 + at : 384 + at]
         ).reshape(23, 8, 128)
 
-    along, deep = lax.div(chan, 4), lax.rem(lax.div(chan, 2), 2)
-
-    def peer(dy, dz, c):
-        return lax.rem(along + dy, 4) * 4 + lax.rem(deep + dz, 2) * 2 + c
-
     def piece_of(ref, g, first, count):
         start, rows = CHUNKS[g]
         return ref.at[pl.ds(first, count), pl.ds(start, rows)]
@@ -224,7 +229,7 @@
         blocks(g, every, every, 0, 0, count, kind, sibling).wait_recv()
 
     t3[:, 7] = jnp.zeros((2, 8, 128), F32)
-    for g in range(3):
+    for g in (1, 2, 0):
         for order in ((0,), (1, 2), (3, 4))[g]:
             for degree in range(LEAST[order], 7):
                 width = 2 * degree + 1
@@ -244,7 +249,7 @@
         for copy in own_sends(g):
             copy.start()
 
-    for g in range(3):
+    for g in (1, 2, 0):
         landed(g, 1, 2)
         passed(g, 0).start()
         passed(g, 1).start()
@@ -261,7 +266,7 @@
     pushes[:, 256:384] = (nconst[0].astype(F32) - nconst[1].astype(F32)).T.astype(BF16)
     for copy in weights:
         copy.wait_recv()
-    for g in range(3):
+    for g in (1, 2, 0):
         landed(g, 0, 11)
         first, rows = CHUNKS[g]
         for t in range(first, first + rows, 16):
@@ -340,47 +345,45 @@
         block = edge_grads[:, 128 * half : 128 * half + 128].reshape(49, 8, 128)
         parts.append(jnp.sum(jnp.sum(block * pt[half], axis=0), axis=0, keepdims=True))
     parts.append(jnp.sum(energy, axis=0, keepdims=True))
-    red[chan] = jnp.concatenate(parts + [jnp.zeros((5, 128), F32)], axis=0)
-
-    def sums(d):
-        to = lax.rem(chan + d, NC)
-        return remote(red.at[chan], red.at[chan], r_send, r_recv, (space, to))
-
-    def launch_sums(d, carry):
-        sums(d).start()
-        return carry
-
-    all_sums = remote(red.at[pl.ds(0, NC - 1)], red.at[pl.ds(0, NC - 1)], r_send, r_recv, (space, sibling))
-    lax.fori_loop(1, NC, launch_sums, 0)
+    pull = jnp.concatenate(parts[:2], axis=1)
+    push = jnp.concatenate([pull * u for u in unit] + [jnp.zeros((5, 256), F32)], axis=0)
+    hi, lo = split(push)
+    hilo = jnp.concatenate([hi.astype(F32), lo.astype(F32)], axis=0).astype(BF16)
+    part = dot(hilo, pushes[...])
+    part = part[0:8] + part[8:16]
+    rank = lax.broadcasted_iota(jnp.int32, (8, 128), 0)
+    fsend[0] = part[:, 0:128]
+    fsend[1] = part[:, 128:256]
+    fsend[2] = jnp.where(rank == 3, parts[2], part[:, 256:384])
+    halves = remote(fsend, frecv, f_send, f_recv, (space, sibling))
+    halves.start()
     both_ghosts.wait_send()
     both_tables.wait_send()
     for copy in weights + [swap]:
         copy.wait_send()
     whole = every.at[pl.ds(0, NC - 1)]
     remote(whole, whole, a_send, a_recv.at[0, 0], (space, sibling)).wait_send()
+    halves.wait_recv()
+    fsum[...] = fsend[...] + frecv[...]
+    red[chip] = fsum[2]
+
+    def deliver(side, slot, where):
+        remote(fsum.at[side], red.at[slot], r_send, r_recv, where).start()
+
+    for d in range(8):
+        to = lax.rem(chip + 4 + d, 8) * 2 + core
+        deliver(0, 8 + chip, (before, to))
+        deliver(1, 16 + chip, (after, to))
+    for d in (4, 3, 5, 2, 6, 1, 7):
+        deliver(2, chip, (space, lax.rem(chip + d, 8) * 2 + core))
+    most = red.at[pl.ds(0, 23)]
+    all_sums = remote(most, most, r_send, r_recv, (space, sibling))
     all_sums.wait_recv()
     summed = jnp.sum(red[...], axis=0)
-    energy_out[...] = summed[2:3]
-    pull = jnp.concatenate([summed[0:1], summed[1:2]], axis=1)
-    push = jnp.concatenate([pull * u for u in unit] + [jnp.zeros((5, 256), F32)], axis=0)
-    hi, lo = split(push)
-    hilo = jnp.concatenate([hi.astype(F32), lo.astype(F32)], axis=0).astype(BF16)
-    part = dot(hilo, pushes[...])
-    part = part[0:8] + part[8:16]
-    fsend[0] = part[:, 0:128]
-    fsend[1] = part[:, 128:256]
-    back = [
-        remote(fsend.at[0], frecv.at[0], f_send, f_recv, (before, chan)),
-        remote(fsend.at[1], frecv.at[1], f_send, f_recv, (after, chan)),
-    ]
-    for copy in back:
-        copy.start()
-    both_back = remote(fsend, frecv, f_send, f_recv, (before, chan))
+    energy_out[...] = summed[3:4]
+    force_out[...] = summed[0:3]
+    halves.wait_send()
     all_sums.wait_send()
-    both_back.wait_recv()
-    force_out[...] = (part[:, 256:384] + frecv[0] + frecv[1])[0:3]
-
-    both_back.wait_send()
 
 
 def local(
@@ -437,9 +440,10 @@
             pltpu.VMEM((2, 128, 256), BF16),
             pltpu.VMEM((256, 384), BF16),
             pltpu.VMEM((7, 8, 128), F32),
-            pltpu.VMEM((NC, 8, 128), F32),
-            pltpu.VMEM((2, 8, 128), F32),
-            pltpu.VMEM((2, 8, 128), F32),
+            pltpu.VMEM((24, 8, 128), F32),
+            pltpu.VMEM((3, 8, 128), F32),
+            pltpu.VMEM((3, 8, 128), F32),
+            pltpu.VMEM((3, 8, 128), F32),
             dma((2,)),
             dma((2,)),
             dma((3,)),

time: 40.4 us -> 39 us (0.965)
  Pallas kernels: 37.2 us -> 35.9 us
    pallas_call x1, Pallas kernels: 37.2 us -> 35.9 us  [local(): pl.pallas_call(kernel, out_shape=(jax.ShapeDtypeStruct((1, 128), F32), ja...]
where the time goes in v3:
time: 39 us; the launch traced here: 38.9 us
  Pallas kernels  35.9 us (92%)
  local copies, waits for them, and re-layouts  1.71 us (4%)
  between operations  1.31 us (3%)
    pallas_call x1, Pallas kernels, local(): pl.pallas_call(kernel, out_shape=(jax.ShapeDtypeStruct((1, 128), F32), ja...  35.9 us
    unnamed x6, local copies, waits for them, and re-layouts  1.71 us

profile of v3, /device:TPU:1, one launch (start us, length us, event | category | flops | bytes accessed | tf_op | source)
XLA Modules:
  0.0 38.9 jit_solution(189937458123651723)
XLA Ops:
  1.3 35.9 %shard_map.140 = (f32[1,128]{1,0:T(1,128)}, f32[3,128]{1,0:T(4,128)}) custom-call(bf16[49,8,128]{2,1,0:T(8,128)(2,1)} %refs_0_.1, s32[2,64]{1,0:T(2,128)} %refs_1_.1, s32[1,256]{1,0:T(1,128)} %bitcast.4, s32[1,256]{1,0:T(1,128)} %bitcast.5, s32[1]{0:T(128)S(6)} %copy.17.refs_4_, bf16[235,256]{1,0:T(8,128)(2,1)} %refs_5_.1, f32[2,128]{1,0:T(2,128)} %bitcast.6, ...), custom_call_target="tpu_custom_call" | custom-call | flops 400000000 | bytes 3000000 | tf_op jit(solution)/shard_map/pallas_call | solution.py:410
  37.2 0.0 copy-start.1
  37.2 0.0 copy-start
  37.2 0.6 %copy-done.1 = f32[1,128]{1,0:T(1,128)S(1)} copy-done((f32[1,128]{1,0:T(1,128)S(1)}, f32[1,128]{1,0:T(1,128)}, u32[]{:S(2)}) %copy-start.1) | copy-done | bytes 536
  37.8 0.5 %copy.18 = f32[128]{0:T(128)} copy(f32[128]{0:T(128)S(1)} %bitcast.7) | data formatting | bytes 1024
  38.3 0.0 copy-done
  38.3 0.6 %copy.19 = f32[3,128]{1,0:T(4,128)} copy(f32[3,128]{1,0:T(4,128)S(1)} %copy-done) | data formatting | bytes 3072
Async XLA Ops:
  37.2 0.6 %copy-start.1 = (f32[1,128]{1,0:T(1,128)S(1)}, f32[1,128]{1,0:T(1,128)}, u32[]{:S(2)}) copy-start(f32[1,128]{1,0:T(1,128)} %get-tuple-element.4) | copy-start | bytes 1540
  37.2 1.1 %copy-start = (f32[3,128]{1,0:T(4,128)S(1)}, f32[3,128]{1,0:T(4,128)}, u32[]{:S(2)}) copy-start(f32[3,128]{1,0:T(4,128)} %get-tuple-element.9) | copy-start | bytes 4612

commit v4 on v3

--- a/solution.py
+++ b/solution.py
@@ -205,13 +205,12 @@
         )
 
     def own_sends(g):
-        plans = [(sibling, other, 0)]
+        plans = []
+        plans += [(peer(2, 0, c), c, 2) for c in range(2)]
+        plans += [(peer(0, 1, c), c, 1) for c in range(2)]
         for c in range(2):
-            plans.append((peer(0, 1, c), c, 1))
-        for c in range(2):
-            plans.append((peer(2, 0, c), c, 2))
-            plans.append((peer(1, 0, c), c, 0))
-            plans.append((peer(3, 0, c), c, 0))
+            plans += [(peer(1, 0, c), c, 0), (peer(3, 0, c), c, 0)]
+        plans += [(sibling, other, 0)]
         return [blocks(g, snd, every, half, chan, 1, kind, to) for to, half, kind in plans]
 
     ahead, behind, across = peer(1, 0, core), peer(3, 0, core), peer(0, 1, core)

time: 39 us -> 37.8 us (0.969)
  Pallas kernels: 35.9 us -> 34.5 us
    pallas_call x1, Pallas kernels: 35.9 us -> 34.5 us  [local(): pl.pallas_call(kernel, out_shape=(jax.ShapeDtypeStruct((1, 128), F32), ja...]
where the time goes in v4:
time: 37.8 us; the launch traced here: 37.5 us
  Pallas kernels  34.5 us (91%)
  local copies, waits for them, and re-layouts  1.71 us (5%)
  between operations  1.31 us (3%)
    pallas_call x1, Pallas kernels, local(): pl.pallas_call(kernel, out_shape=(jax.ShapeDtypeStruct((1, 128), F32), ja...  34.5 us
    unnamed x6, local copies, waits for them, and re-layouts  1.71 us

profile of v4, /device:TPU:1, one launch (start us, length us, event | category | flops | bytes accessed | tf_op | source)
XLA Modules:
  0.0 37.5 jit_solution(405827731983414224)
XLA Ops:
  1.3 34.5 %shard_map.140 = (f32[1,128]{1,0:T(1,128)}, f32[3,128]{1,0:T(4,128)}) custom-call(bf16[49,8,128]{2,1,0:T(8,128)(2,1)} %refs_0_.1, s32[2,64]{1,0:T(2,128)} %refs_1_.1, s32[1,256]{1,0:T(1,128)} %bitcast.4, s32[1,256]{1,0:T(1,128)} %bitcast.5, s32[1]{0:T(128)S(6)} %copy.17.refs_4_, bf16[235,256]{1,0:T(8,128)(2,1)} %refs_5_.1, f32[2,128]{1,0:T(2,128)} %bitcast.6, ...), custom_call_target="tpu_custom_call" | custom-call | flops 400000000 | bytes 3000000 | tf_op jit(solution)/shard_map/pallas_call | solution.py:409
  35.8 0.0 copy-start.1
  35.8 0.0 copy-start
  35.8 0.6 %copy-done.1 = f32[1,128]{1,0:T(1,128)S(1)} copy-done((f32[1,128]{1,0:T(1,128)S(1)}, f32[1,128]{1,0:T(1,128)}, u32[]{:S(2)}) %copy-start.1) | copy-done | bytes 536
  36.4 0.5 %copy.18 = f32[128]{0:T(128)} copy(f32[128]{0:T(128)S(1)} %bitcast.7) | data formatting | bytes 1024
  36.9 0.0 copy-done
  36.9 0.6 %copy.19 = f32[3,128]{1,0:T(4,128)} copy(f32[3,128]{1,0:T(4,128)S(1)} %copy-done) | data formatting | bytes 3072
Async XLA Ops:
  35.8 0.6 %copy-start.1 = (f32[1,128]{1,0:T(1,128)S(1)}, f32[1,128]{1,0:T(1,128)}, u32[]{:S(2)}) copy-start(f32[1,128]{1,0:T(1,128)} %get-tuple-element.4) | copy-start | bytes 1540
  35.8 1.1 %copy-start = (f32[3,128]{1,0:T(4,128)S(1)}, f32[3,128]{1,0:T(4,128)}, u32[]{:S(2)}) copy-start(f32[3,128]{1,0:T(4,128)} %get-tuple-element.9) | copy-start | bytes 4612

commit v5 on v4

--- a/solution.py
+++ b/solution.py
@@ -228,7 +228,7 @@
         blocks(g, every, every, 0, 0, count, kind, sibling).wait_recv()
 
     t3[:, 7] = jnp.zeros((2, 8, 128), F32)
-    for g in (1, 2, 0):
+    for g in (2, 1, 0):
         for order in ((0,), (1, 2), (3, 4))[g]:
             for degree in range(LEAST[order], 7):
                 width = 2 * degree + 1
@@ -248,7 +248,7 @@
         for copy in own_sends(g):
             copy.start()
 
-    for g in (1, 2, 0):
+    for g in (2, 1, 0):
         landed(g, 1, 2)
         passed(g, 0).start()
         passed(g, 1).start()
@@ -265,7 +265,7 @@
     pushes[:, 256:384] = (nconst[0].astype(F32) - nconst[1].astype(F32)).T.astype(BF16)
     for copy in weights:
         copy.wait_recv()
-    for g in (1, 2, 0):
+    for g in (2, 1, 0):
         landed(g, 0, 11)
         first, rows = CHUNKS[g]
         for t in range(first, first + rows, 16):

time: 37.8 us -> 37.7 us (level)
  no operation moved by 1% of the time
where the time goes in v5:
time: 37.7 us; the launch traced here: 37.4 us
  Pallas kernels  34.4 us (91%)
  local copies, waits for them, and re-layouts  1.71 us (5%)
  between operations  1.31 us (3%)
    pallas_call x1, Pallas kernels, local(): pl.pallas_call(kernel, out_shape=(jax.ShapeDtypeStruct((1, 128), F32), ja...  34.4 us
    unnamed x6, local copies, waits for them, and re-layouts  1.71 us

profile of v5, /device:TPU:1, one launch (start us, length us, event | category | flops | bytes accessed | tf_op | source)
XLA Modules:
  0.0 37.4 jit_solution(2000419405669963799)
XLA Ops:
  1.3 34.4 %shard_map.140 = (f32[1,128]{1,0:T(1,128)}, f32[3,128]{1,0:T(4,128)}) custom-call(bf16[49,8,128]{2,1,0:T(8,128)(2,1)} %refs_0_.1, s32[2,64]{1,0:T(2,128)} %refs_1_.1, s32[1,256]{1,0:T(1,128)} %bitcast.4, s32[1,256]{1,0:T(1,128)} %bitcast.5, s32[1]{0:T(128)S(6)} %copy.17.refs_4_, bf16[235,256]{1,0:T(8,128)(2,1)} %refs_5_.1, f32[2,128]{1,0:T(2,128)} %bitcast.6, ...), custom_call_target="tpu_custom_call" | custom-call | flops 400000000 | bytes 3000000 | tf_op jit(solution)/shard_map/pallas_call | solution.py:409
  35.7 0.0 copy-start.1
  35.7 0.0 copy-start
  35.7 0.6 %copy-done.1 = f32[1,128]{1,0:T(1,128)S(1)} copy-done((f32[1,128]{1,0:T(1,128)S(1)}, f32[1,128]{1,0:T(1,128)}, u32[]{:S(2)}) %copy-start.1) | copy-done | bytes 536
  36.4 0.5 %copy.18 = f32[128]{0:T(128)} copy(f32[128]{0:T(128)S(1)} %bitcast.7) | data formatting | bytes 1024
  36.9 0.0 copy-done
  36.9 0.6 %copy.19 = f32[3,128]{1,0:T(4,128)} copy(f32[3,128]{1,0:T(4,128)S(1)} %copy-done) | data formatting | bytes 3072
Async XLA Ops:
  35.7 0.6 %copy-start.1 = (f32[1,128]{1,0:T(1,128)S(1)}, f32[1,128]{1,0:T(1,128)}, u32[]{:S(2)}) copy-start(f32[1,128]{1,0:T(1,128)} %get-tuple-element.4) | copy-start | bytes 1540
  35.7 1.1 %copy-start = (f32[3,128]{1,0:T(4,128)S(1)}, f32[3,128]{1,0:T(4,128)}, u32[]{:S(2)}) copy-start(f32[3,128]{1,0:T(4,128)} %get-tuple-element.9) | copy-start | bytes 4612

commit v6 on v5

--- a/solution.py
+++ b/solution.py
@@ -245,9 +245,12 @@
             )
         every[chan, first : first + rows] = snd[core, first : first + rows]
 
-        for copy in own_sends(g):
+        for copy in own_sends(g)[:4]:
             copy.start()
 
+    for g in (2, 1, 0):
+        for copy in own_sends(g)[4:]:
+            copy.start()
     for g in (2, 1, 0):
         landed(g, 1, 2)
         passed(g, 0).start()

time: 37.7 us -> 37.8 us (level)
  no operation moved by 1% of the time
where the time goes in v6:
time: 37.8 us; the launch traced here: 37.7 us
  Pallas kernels  34.7 us (92%)
  local copies, waits for them, and re-layouts  1.71 us (5%)
  between operations  1.31 us (3%)
    pallas_call x1, Pallas kernels, local(): pl.pallas_call(kernel, out_shape=(jax.ShapeDtypeStruct((1, 128), F32), ja...  34.7 us
    unnamed x6, local copies, waits for them, and re-layouts  1.71 us

profile of v6, /device:TPU:1, one launch (start us, length us, event | category | flops | bytes accessed | tf_op | source)
XLA Modules:
  0.0 37.7 jit_solution(12376481154762042352)
XLA Ops:
  1.3 34.7 %shard_map.140 = (f32[1,128]{1,0:T(1,128)}, f32[3,128]{1,0:T(4,128)}) custom-call(bf16[49,8,128]{2,1,0:T(8,128)(2,1)} %refs_0_.1, s32[2,64]{1,0:T(2,128)} %refs_1_.1, s32[1,256]{1,0:T(1,128)} %bitcast.4, s32[1,256]{1,0:T(1,128)} %bitcast.5, s32[1]{0:T(128)S(6)} %copy.17.refs_4_, bf16[235,256]{1,0:T(8,128)(2,1)} %refs_5_.1, f32[2,128]{1,0:T(2,128)} %bitcast.6, ...), custom_call_target="tpu_custom_call" | custom-call | flops 400000000 | bytes 3000000 | tf_op jit(solution)/shard_map/pallas_call | solution.py:412
  36.0 0.0 copy-start.1
  36.0 0.0 copy-start
  36.0 0.6 %copy-done.1 = f32[1,128]{1,0:T(1,128)S(1)} copy-done((f32[1,128]{1,0:T(1,128)S(1)}, f32[1,128]{1,0:T(1,128)}, u32[]{:S(2)}) %copy-start.1) | copy-done | bytes 536
  36.6 0.5 %copy.18 = f32[128]{0:T(128)} copy(f32[128]{0:T(128)S(1)} %bitcast.7) | data formatting | bytes 1024
  37.1 0.0 copy-done
  37.1 0.6 %copy.19 = f32[3,128]{1,0:T(4,128)} copy(f32[3,128]{1,0:T(4,128)S(1)} %copy-done) | data formatting | bytes 3072
Async XLA Ops:
  36.0 0.6 %copy-start.1 = (f32[1,128]{1,0:T(1,128)S(1)}, f32[1,128]{1,0:T(1,128)}, u32[]{:S(2)}) copy-start(f32[1,128]{1,0:T(1,128)} %get-tuple-element.4) | copy-start | bytes 1540
  36.0 1.1 %copy-start = (f32[3,128]{1,0:T(4,128)S(1)}, f32[3,128]{1,0:T(4,128)}, u32[]{:S(2)}) copy-start(f32[3,128]{1,0:T(4,128)} %get-tuple-element.9) | copy-start | bytes 4612
